TPU v7x, 128 devices: a whole 4x4x4 slice. The times are simulated.
128 devices in a mesh: mem: 8 (over z, core), col: 16 (over x, y).
Axes of the slice: x: 4, y: 4, z: 4, core: 2. Of those that a mesh axis runs over, the one named last changes fastest.
Arguments:
- prior_trajectory: bfloat16 [94, 1024, 1024], P(None, 'col', 'mem'), may hold values from -6 to 6
- predicted_measurements: bfloat16 [4096, 128, 1024], P('col', None, 'mem'), may hold values from -6 to 6
- departure_vector: float32 [4096, 128], replicated, may hold values from -6 to 6
- measurement_error_spread: float32 [4096, 128], replicated, may hold values from 0.01 to 1
- valid_tallies: int32 [4096], replicated, may hold values from 1 to 128
- area_point_sequence: int32 [1024], P('col'), may hold values from 0 to 63, as said below
- nearby_batch_map: int32 [128, 3, 3], replicated, may hold values from 0 to 255, as said below
Outputs:
- analysis: bfloat16 [94, 1024, 1024], P(None, ('mem', 'col'))
Inputs may be any that keep to these rules, and one draw needn't show every extreme that they name: `area_point_sequence`: each aligned block of 64 entries, one region's, holds every number 0 to 63 once. `nearby_batch_map`: the 3 entries of one group and slot are different.
All inputs are finite; a program needn't handle non-finite values.
Results may differ from a plain program's by a relative error of at most 0.009.
The roundings to bfloat16 on the way count: a program that leaves them out, or rounds other values in their place, can miss the bound.
Values may be sent and summed in bfloat16 or wider, within the bound.
A program may use at most 128 MiB of HBM per device.

v0:
```python
import jax
import jax.numpy as jnp
from jax import lax
from jax.sharding import PartitionSpec as P

NS_ITERS = 5


def extended(x, sides, width):
    for axis, dim in sides:
        peers, length = (lax.axis_size(axis), x.shape[dim])
        up = [(i, (i + 1) % peers) for i in range(peers)]
        down = [(j, i) for i, j in up]
        last = lax.slice_in_dim(x, length - width, length, axis=dim)
        first = lax.slice_in_dim(x, 0, width, axis=dim)
        before = lax.ppermute(last, axis, up)
        after = lax.ppermute(first, axis, down)
        x = jnp.concatenate([before, x, after], axis=dim)
    return x


def analyse(model_quantities, obs_rows, innov_rows, var_rows, count_rows):
    members = obs_rows.shape[1]
    slots = innov_rows.shape[1]
    valid_mask = (jnp.arange(slots, dtype=jnp.int32)[None, :] < count_rows[:, None]).astype(
        jnp.float32
    )
    root_w = (valid_mask * lax.rsqrt(var_rows)).reshape(-1, 1)
    obs_mean = jnp.sum(obs_rows, axis=1, dtype=jnp.float32, keepdims=True) / members
    scaled = ((obs_rows - obs_mean) * root_w).astype(jnp.bfloat16)
    cross = lax.dot_general(
        scaled, scaled, (((0,), (0,)), ((), ())), preferred_element_type=jnp.float32
    )
    identity = jnp.eye(members, dtype=jnp.float32)
    system = cross + (members - 1.0) * identity
    bound = members - 1.0 + jnp.sqrt(jnp.sum(cross * cross))
    drive_vec = (innov_rows.reshape(-1, 1) * root_w).astype(jnp.bfloat16)
    projected = lax.dot_general(
        scaled, drive_vec, (((0,), (0,)), ((), ())), preferred_element_type=jnp.float32
    )[:, 0]
    root_iter = (system / bound).astype(jnp.bfloat16)
    inverse = root_iter
    for sweep in range(NS_ITERS):
        if sweep == 0:
            factor = ((3.0 * identity - root_iter) * 0.5).astype(jnp.bfloat16)
            inverse = factor
        else:
            product = jnp.dot(inverse, root_iter, preferred_element_type=jnp.float32)
            factor = ((3.0 * identity - product) * 0.5).astype(jnp.bfloat16)
            inverse = jnp.dot(factor, inverse, preferred_element_type=jnp.float32).astype(
                jnp.bfloat16
            )
        if sweep + 1 < NS_ITERS:
            root_iter = jnp.dot(root_iter, factor, preferred_element_type=jnp.float32).astype(
                jnp.bfloat16
            )
    inverse_f = inverse.astype(jnp.float32)
    half_step = jnp.dot(inverse_f, projected, precision=lax.Precision.HIGHEST)
    mean_w = jnp.dot(inverse_f, half_step, precision=lax.Precision.HIGHEST) / bound
    weights = (jnp.sqrt((members - 1.0) / bound) * inverse_f + mean_w[:, None]).astype(jnp.bfloat16)
    layer_indices = model_quantities.shape[0]
    group_column_list = model_quantities.shape[1]
    flat_state = model_quantities.reshape(layer_indices * group_column_list, members)
    state_mean = jnp.sum(flat_state, axis=1, dtype=jnp.float32, keepdims=True) / members
    spread = (flat_state - state_mean).astype(jnp.bfloat16)
    result = state_mean + jnp.dot(spread, weights, preferred_element_type=jnp.float32)
    return result.astype(jnp.bfloat16).reshape(layer_indices, group_column_list, members)


def body(
    prior_trajectory,
    predicted_measurements,
    departure_vector,
    measurement_error_spread,
    valid_tallies,
    area_point_sequence,
    nearby_batch_map,
):
    group_member_states = lax.axis_size("mem")
    regions = lax.axis_size("col")
    mem_index = lax.axis_index("mem")
    col_index = lax.axis_index("col")
    layer_indices = prior_trajectory.shape[0]
    area_point_indices = prior_trajectory.shape[1]
    group_column_list = area_point_indices // group_member_states
    local_blocks = predicted_measurements.shape[0]
    slots = predicted_measurements.shape[1]
    per_slot = nearby_batch_map.shape[2]
    chosen_batches = jnp.take(prior_trajectory, area_point_sequence, axis=1).reshape(
        layer_indices, group_member_states, group_column_list, -1
    )
    model_quantities = lax.all_to_all(
        chosen_batches, "mem", split_axis=1, concat_axis=3, tiled=True
    ).reshape(layer_indices, group_column_list, -1)
    pattern_rows = nearby_batch_map.reshape(group_member_states, regions, 3, per_slot)
    nearby = extended(predicted_measurements, (("col", 0),), local_blocks)
    own_pattern = lax.dynamic_index_in_dim(pattern_rows, col_index, 1, keepdims=False)
    offsets = jnp.arange(3, dtype=jnp.int32)[None, :, None] * local_blocks
    block_ids = (own_pattern + offsets).reshape(-1)
    chosen = jnp.take(nearby, block_ids, axis=0).reshape(
        group_member_states, 3 * per_slot, slots, -1
    )
    gathered = lax.all_to_all(chosen, "mem", split_axis=0, concat_axis=3, tiled=True)
    obs_rows = gathered.reshape(-1, gathered.shape[-1])
    group_id = mem_index * regions + col_index
    group_pattern = lax.dynamic_index_in_dim(nearby_batch_map, group_id, 0, keepdims=False)
    regions_of = (col_index + jnp.arange(3, dtype=jnp.int32) - 1 + regions) % regions
    blocks = (regions_of[:, None] * local_blocks + group_pattern).reshape(-1)
    innov_rows = jnp.take(departure_vector, blocks, axis=0)
    var_rows = jnp.take(measurement_error_spread, blocks, axis=0)
    count_rows = jnp.take(valid_tallies, blocks, axis=0)
    return analyse(model_quantities, obs_rows, innov_rows, var_rows, count_rows)


def solution(mesh):
    in_specs = (P(None, "col", "mem"), P("col", None, "mem"), P(), P(), P(), P("col"), P())
    out_specs = P(None, ("mem", "col"), None)
    return jax.shard_map(body, mesh=mesh, in_specs=in_specs, out_specs=out_specs, check_vma=False)
```

profile of v0, /device:TPU:1, one launch (start us, length us, event | category | flops | bytes accessed | tf_op | source)
XLA Modules:
  0.0 319.1 jit_solution(14459433030153363656)
XLA Ops:
  0.0 5.8 %collective-permute-start.1 = (bf16[256,128,128]{2,1,0:T(8,128)(2,1)}, bf16[256,128,128]{2,1,0:T(8,128)(2,1)}, u32[]{:S(2)}, u32[]{:S(2)}) collective-permute-start(bf16[256,128,128]{2,1,0:T(8,128)(2,1)} %param.10), channel_id=1, source_target_pairs={{1,0},{2,1},{3,2},{4,3},{5,4},{6,5},{7,6},{8,7},{9,8},{10,9},{11,1... | collective-permute-start | bytes 25165832 | tf_op jit(solution)/shard_map/ppermute | solution.py:17
  7.2 7.6 %gather_fusion = bf16[64,94,128]{2,0,1:T(8,128)(2,1)} fusion(bf16[94,64,128]{2,1,0:T(8,128)(2,1)} %param.9, s32[1024]{0:T(1024)S(1)} %pad_clamp_fusion.3), kind=kCustom, calls=%fused_computation.2 | custom fusion | bytes 3080448 | tf_op jit(solution)/shard_map/jit(_take)/gather | solution.py:89
  14.8 2.9 copy_select_fusion
  17.7 6.3 %all-to-all-start = ((bf16[94,8,8,128]{3,2,0,1:T(8,128)(2,1)}), bf16[94,8,8,128]{3,2,0,1:T(8,128)(2,1)}, u32[]{:S(2)}, u32[]{:S(2)}) async-start(bf16[94,8,8,128]{3,2,0,1:T(8,128)(2,1)} %copy_select_fusion), calls=%async_computation | async-start | bytes 3080192 | tf_op jit(solution)/shard_map/all_to_all | solution.py:92
  25.1 160.1 %collective-permute-done.1 = bf16[256,128,128]{2,1,0:T(8,128)(2,1)} collective-permute-done((bf16[256,128,128]{2,1,0:T(8,128)(2,1)}, bf16[256,128,128]{2,1,0:T(8,128)(2,1)}, u32[]{:S(2)}, u32[]{:S(2)}) %collective-permute-start.1) | collective-permute-done | bytes 8388640 | tf_op jit(solution)/shard_map/ppermute | solution.py:17
  185.2 5.2 %collective-permute-done = bf16[256,128,128]{2,1,0:T(8,128)(2,1)} collective-permute-done((bf16[256,128,128]{2,1,0:T(8,128)(2,1)}, bf16[256,128,128]{2,1,0:T(8,128)(2,1)}, u32[]{:S(2)}, u32[]{:S(2)}) %collective-permute-start) | collective-permute-done | bytes 8388640 | tf_op jit(solution)/shard_map/ppermute | solution.py:16
  190.4 18.2 %pad_maximum_fusion = bf16[768,128,128]{2,1,0:T(8,128)(2,1)} fusion(bf16[256,128,128]{2,1,0:T(8,128)(2,1)} %collective-permute-done.1, bf16[256,128,128]{2,1,0:T(8,128)(2,1)} %param.10, bf16[256,128,128]{2,1,0:T(8,128)(2,1)} %collective-permute-done), kind=kLoop, calls=%fused_computation.5 | loop fusion | flops 25165824 | bytes 50331648 | tf_op jit(solution)/shard_map/concatenate | solution.py:18
  208.6 10.7 %gather_fusion.1 = bf16[72,128,128]{2,1,0:T(8,128)(2,1)} fusion(bf16[768,128,128]{2,1,0:T(8,128)(2,1)} %pad_maximum_fusion, s32[1024]{0:T(1024)S(1)} %pad_clamp_fusion.2), kind=kCustom, calls=%fused_computation.3 | custom fusion | bytes 4718880 | tf_op jit(solution)/shard_map/jit(_take)/gather | solution.py:100
  219.2 3.4 %broadcast_select_fusion = bf16[8,9,128,128]{3,2,1,0:T(8,128)(2,1)} fusion(bf16[8,9,128,128]{3,2,1,0:T(8,128)(2,1)} %bitcast.90, pred[8,9]{1,0:T(8,128)(4,1)S(1)} %compare_and_fusion), kind=kLoop, calls=%fused_computation.39 | loop fusion | flops 1179648 | bytes 4718664 | tf_op jit(solution)/shard_map/jit(_take)/select_n | solution.py:100
  222.6 7.3 %all-to-all-start.1 = ((bf16[8,9,128,128]{3,2,1,0:T(8,128)(2,1)}), bf16[8,9,128,128]{3,2,1,0:T(8,128)(2,1)}, u32[]{:S(2)}, u32[]{:S(2)}) async-start(bf16[8,9,128,128]{3,2,1,0:T(8,128)(2,1)} %broadcast_select_fusion), calls=%async_computation.1 | async-start | bytes 4718592 | tf_op jit(solution)/shard_map/all_to_all | solution.py:103
  231.1 2.1 gather_fusion.3
  234.1 1.7 convert_reduce_fusion
  235.9 23.3 %all-to-all-done.1 = bf16[8,9,128,128]{3,2,1,0:T(8,128)(2,1)} async-done(((bf16[8,9,128,128]{3,2,1,0:T(8,128)(2,1)}), bf16[8,9,128,128]{3,2,1,0:T(8,128)(2,1)}, u32[]{:S(2)}, u32[]{:S(2)}) %all-to-all-start.1) | async-done | bytes 2359328 | tf_op jit(solution)/shard_map/all_to_all | solution.py:103
  259.1 2.0 fusion.1
  261.2 2.5 fusion.3
  265.4 5.4 %multiply_reduce_fusion = (f32[]{:T(128)}, f32[1024,1024]{1,0:T(8,128)}) fusion(bf16[144,8,8,128]{3,2,1,0:T(8,128)(2,1)S(1)} %bitcast.91), kind=kOutput, calls=%fused_computation.29 | convolution fusion | flops 2418016256 | bytes 6553604 | tf_op jit(solution)/shard_map/dot_general | solution.py:31
  271.5 2.8 divide_convert_fusion
  274.3 2.4 convolution_convert_fusion.5
  276.7 2.4 fusion.7
  279.0 2.4 convolution_convert_fusion.4
  281.4 2.3 convolution_convert_fusion.3
  283.8 2.3 fusion.9
  286.1 2.3 convolution_convert_fusion.2
  288.5 2.6 convolution_convert_fusion.1
  291.1 2.4 fusion.11
  293.5 3.7 %convolution_convert_fusion = bf16[1024,1024]{1,0:T(8,128)(2,1)} fusion(bf16[1024,1024]{1,0:T(8,128)(2,1)S(1)} %fusion.11, bf16[1024,1024]{1,0:T(8,128)(2,1)S(1)} %convolution_convert_fusion.2), kind=kOutput, calls=%fused_computation.52 | convolution fusion | flops 2148532224 | bytes 6291456 | tf_op jit(solution)/shard_map/dot_general | solution.py:50
  297.2 3.7 %fusion.69 = bf16[1024,1024]{1,0:T(8,128)(2,1)} fusion(bf16[1024,1024]{1,0:T(8,128)(2,1)S(1)} %convolution_convert_fusion.1, bf16[1024,1024]{1,0:T(8,128)(2,1)S(1)} %fusion.11), kind=kOutput, calls=%fused_computation.107 | convolution fusion | flops 2147483648 | bytes 6291456 | tf_op jit(solution)/shard_map/dot_general | solution.py:54
  300.9 2.1 fusion.42
  302.9 7.4 %fusion.31 = bf16[1024,1024]{1,0:T(8,128)(2,1)S(1)} fusion(bf16[1024,1024]{1,0:T(8,128)(2,1)} %convolution_convert_fusion, bf16[1024,1024]{1,0:T(8,128)(2,1)} %fusion.69), kind=kOutput, calls=%fused_computation.51 | convolution fusion | flops 4301258752 | bytes 6291456 | tf_op jit(solution)/shard_map/dot_general | solution.py:50
  310.3 1.7 convolution_bitcast_fusion
  312.0 1.7 fusion.70
  313.9 5.2 %fusion.34 = bf16[94,8,1024]{2,1,0:T(8,128)(2,1)} fusion(bf16[1024,1024]{1,0:T(8,128)(2,1)} %copy-done.3, f32[1024]{0:T(1024)S(1)} %broadcast_divide_fusion, f32[]{:T(128)S(6)} %sqrt.7, f32[752]{0:T(1024)S(1)} %div.31, bf16[94,8,8,128]{3,2,0,1:T(8,128)(2,1)} %all-to-all-done), kind=kOutput, calls=%fused_computation.58 | convolution fusion | flops 1585102848 | bytes 5184452 | tf_op jit(solution)/shard_map/dot_general | solution.py:66
  (52 shorter events, 6.2 us)
Async XLA Ops:
  0.0 230.6 %copy-start = (f32[4096,128]{1,0:T(8,128)S(1)}, f32[4096,128]{1,0:T(8,128)}, u32[]{:S(2)}) copy-start(f32[4096,128]{1,0:T(8,128)} %param.11) | copy-start | bytes 6291460
  0.0 185.2 %collective-permute-start.1 = (bf16[256,128,128]{2,1,0:T(8,128)(2,1)}, bf16[256,128,128]{2,1,0:T(8,128)(2,1)}, u32[]{:S(2)}, u32[]{:S(2)}) collective-permute-start(bf16[256,128,128]{2,1,0:T(8,128)(2,1)} %param.10), channel_id=1, source_target_pairs={{1,0},{2,1},{3,2},{4,3},{5,4},{6,5},{7,6},{8,7},{9,8},{10,9},{11,1... | collective-permute-start | bytes 25165832 | tf_op jit(solution)/shard_map/ppermute | solution.py:17
  5.8 184.6 %collective-permute-start = (bf16[256,128,128]{2,1,0:T(8,128)(2,1)}, bf16[256,128,128]{2,1,0:T(8,128)(2,1)}, u32[]{:S(2)}, u32[]{:S(2)}) collective-permute-start(bf16[256,128,128]{2,1,0:T(8,128)(2,1)} %param.10), channel_id=1, source_target_pairs={{0,1},{1,2},{2,3},{3,4},{4,5},{5,6},{6,7},{7,8},{8,9},{9,10},{10,1... | collective-permute-start | bytes 25165832 | tf_op jit(solution)/shard_map/ppermute | solution.py:16
  14.8 9.2 %copy-start.5 = (s32[128,3,3]{0,2,1:T(4,128)S(1)}, s32[128,3,3]{0,2,1:T(4,128)}, u32[]{:S(2)}) copy-start(s32[128,3,3]{0,2,1:T(4,128)} %param.15) | copy-start | bytes 13828
  17.7 204.8 %all-to-all-start = ((bf16[94,8,8,128]{3,2,0,1:T(8,128)(2,1)}), bf16[94,8,8,128]{3,2,0,1:T(8,128)(2,1)}, u32[]{:S(2)}, u32[]{:S(2)}) async-start(bf16[94,8,8,128]{3,2,0,1:T(8,128)(2,1)} %copy_select_fusion), calls=%async_computation | async-start | bytes 3080192 | tf_op jit(solution)/shard_map/all_to_all | solution.py:92
  222.6 10.7 %copy-start.2 = (s32[4096]{0:T(1024)S(1)}, s32[4096]{0:T(1024)}, u32[]{:S(2)}) copy-start(s32[4096]{0:T(1024)} %param.13) | copy-start | bytes 49156
  222.6 36.6 %all-to-all-start.1 = ((bf16[8,9,128,128]{3,2,1,0:T(8,128)(2,1)}), bf16[8,9,128,128]{3,2,1,0:T(8,128)(2,1)}, u32[]{:S(2)}, u32[]{:S(2)}) async-start(bf16[8,9,128,128]{3,2,1,0:T(8,128)(2,1)} %broadcast_select_fusion), calls=%async_computation.1 | async-start | bytes 4718592 | tf_op jit(solution)/shard_map/all_to_all | solution.py:103
  265.4 5.4 %copy-start.4 = (bf16[1,9,128,8,128]{4,3,2,1,0:T(8,128)(2,1)}, bf16[1,9,128,8,128]{4,3,2,1,0:T(8,128)(2,1)S(1)}, u32[]{:S(2)}) copy-start(bf16[1,9,128,8,128]{4,3,2,1,0:T(8,128)(2,1)S(1)} %copy.25) | copy-start | bytes 7077892
  310.3 1.7 copy-start.3
  313.8 5.2 %copy-start.1 = (f32[4096,128]{1,0:T(8,128)S(1)}, f32[4096,128]{1,0:T(8,128)}, u32[]{:S(2)}) copy-start(f32[4096,128]{1,0:T(8,128)} %param.11) | copy-start | bytes 6291460
where the time goes:
time: 320 us; the launch traced here: 319 us
  waiting for transfers between devices  189 us (59%)
  matrix products  50 us (16%)
  other arithmetic  35 us (11%)
  local copies, waits for them, and re-layouts  25.1 us (8%)
  starting transfers between devices  19.3 us (6%)
    ppermute x1, waiting for transfers between devices, extended(): after = lax.ppermute(first, axis, down)  160 us
    all_to_all x1, waiting for transfers between devices, body(): lax.all_to_all(chosen, 'mem', split_axis=0, concat_axis=3, tiled=True)  23.3 us
    concatenate x1, other arithmetic, extended(): x = jnp.concatenate([before, x, after], axis=dim)  18.2 us
    dot_general x4, matrix products, analyse(): jnp.dot(factor, inverse, preferred_element_type=jnp.float32)  15.8 us
    dot_general x4, matrix products, analyse(): jnp.dot(root_iter, factor, preferred_element_type=jnp.float32)  11 us
    gather x1, local copies, waits for them, and re-layouts, body(): jnp.take(nearby, block_ids, axis=0)  10.7 us
    gather x1, local copies, waits for them, and re-layouts, body(): jnp.take(prior_trajectory, area_point_sequence, axis=1)  7.64 us
    all_to_all x1, starting transfers between devices, body(): lax.all_to_all(chosen, 'mem', split_axis=0, concat_axis=3, tiled=True)  7.31 us
  transfers between devices with their start and end apart: 4, of which 3 were waited for; matrix products, arithmetic and copies ran while one was open for 16% of the time, Pallas kernels for 0%

commit v1 on v0

v1 whole, which is shorter than its diff:
```python
import jax
import jax.numpy as jnp
from jax import lax
from jax.experimental import pallas as pl
from jax.experimental.pallas import tpu as pltpu
from jax.sharding import PartitionSpec as P

NS_ITERS = 5
N_MEM, N_COL = 8, 16
K = 1024
LAYERS, CD, SLAB = 94, 8, 64
STATE_ROWS = LAYERS * CD
OBR, BLK, NPER = 256, 128, 3
SLOT_ROWS = NPER * BLK
OBS_ROWS = 3 * SLOT_ROWS
LANES = K // N_MEM
B = 256
NB = K // B
LOADS = 8
STATE_CUTS = (0, 256, 512, 752)
MESH = pl.DeviceIdType.MESH
f32, bf16 = jnp.float32, jnp.bfloat16


def unit_block():
    row = lax.broadcasted_iota(jnp.int32, (B, B), 0)
    column = lax.broadcasted_iota(jnp.int32, (B, B), 1)
    return jnp.where(row == column, 1.0, 0.0).astype(f32)


def span(i):
    return slice(i * B, (i + 1) * B)


def put_pair(dst, i, j, tile):
    dst[span(i), span(j)] = tile
    if i != j:
        dst[span(j), span(i)] = tile.T


def halved(tile, diagonal):
    return (3.0 * unit_block() - tile) * 0.5 if diagonal else tile * -0.5


def symmetric_dot(a, b, dst, as_factor=False):
    for j in range(NB):
        for i in range(j + 1):
            tile = jnp.dot(a[span(i), :], b[:, span(j)], preferred_element_type=f32)
            if as_factor:
                tile = halved(tile, i == j)
            put_pair(dst, i, j, tile.astype(bf16))


def precise_row_times(row, matrix):
    high = row.astype(bf16).astype(f32)
    middle = (row - high).astype(bf16).astype(f32)
    low = row - high - middle
    place = lax.broadcasted_iota(jnp.int32, row.shape, 0)
    terms = jnp.where(place == 0, high, jnp.where(place == 1, middle, jnp.where(place == 2, low, 0.0)))
    product = jnp.dot(terms.astype(bf16), matrix[...], preferred_element_type=f32)
    return jnp.broadcast_to(jnp.sum(product, axis=0, keepdims=True), product.shape)


def kernel(
    prior_hbm, obs_hbm, departure_hbm, variance_hbm, counts, sequence, nearby, out_hbm,
    prior, obs, departure, variance, outgoing, rows, states_out, states, scaled, scaled_t,
    cross, root_a, root_b, inverse_a, inverse_b, factor, spread, result, pick, drive,
    load_sem, obs_send, obs_recv, state_send, state_recv, out_sem,
):
    m = lax.axis_index("mem")
    c = lax.axis_index("col")

    def column_of(s):
        return lax.rem(c - s + 1 + N_COL, N_COL)

    def member(dz, dk):
        return lax.rem(m // 2 + dz, 4) * 2 + lax.rem(lax.rem(m, 2) + dk, 2)

    hops = [(dz, dk) for dz in (1, 3, 2, 0) for dk in (0, 1)]
    partners = [(s, dz, dk) for s in (1, 0, 2) for dz, dk in hops if (s, dz, dk) != (1, 0, 0)]

    barrier = pltpu.get_barrier_semaphore()
    for s, dz, dk in partners:
        pl.semaphore_signal(
            barrier, inc=1, device_id={"mem": member(dz, dk), "col": column_of(s)}, device_id_type=MESH
        )

    loads = []
    part = OBR // LOADS
    for i in range(LOADS):
        cut = pl.ds(i * part, part)
        loads.append(pltpu.make_async_copy(obs_hbm.at[cut], obs.at[cut], load_sem.at[i]))
    for s in range(3):
        region = lax.rem(c + s - 1 + N_COL, N_COL)
        cut = pl.ds(pl.multiple_of(region * OBR, OBR), OBR)
        loads.append(pltpu.make_async_copy(departure_hbm.at[cut], departure.at[s], load_sem.at[LOADS + 2 * s]))
        loads.append(pltpu.make_async_copy(variance_hbm.at[cut], variance.at[s], load_sem.at[LOADS + 2 * s + 1]))
    loads.append(pltpu.make_async_copy(prior_hbm, prior, load_sem.at[LOADS + 6]))
    for copy in loads:
        copy.start()
    for copy in loads[:LOADS]:
        copy.wait()

    def block_index(group_m, group_c, s, k):
        return nearby[s, k, group_m * N_COL + group_c]

    for k in range(NPER):
        at = SLOT_ROWS + k * BLK
        rows[m, at : at + BLK, :] = obs[block_index(m, c, 1, k)]
    pl.semaphore_wait(barrier, len(partners))
    obs_copies = []
    for n, (s, dz, dk) in enumerate(partners):
        to_m, to_c = member(dz, dk), column_of(s)
        for k in range(NPER):
            outgoing[n, k * BLK : (k + 1) * BLK, :] = obs[block_index(to_m, to_c, s, k)]
        copy = pltpu.make_async_remote_copy(
            src_ref=outgoing.at[n],
            dst_ref=rows.at[m, pl.ds(s * SLOT_ROWS, SLOT_ROWS)],
            send_sem=obs_send.at[n],
            recv_sem=obs_recv.at[s * N_MEM + m],
            device_id={"mem": to_m, "col": to_c},
            device_id_type=MESH,
        )
        copy.start()
        obs_copies.append(copy)

    def wait_obs(s):
        for dz, dk in hops:
            if (s, dz, dk) != (1, 0, 0):
                source = member(dz, dk)
                pltpu.make_async_remote_copy(
                    src_ref=outgoing.at[0],
                    dst_ref=rows.at[source, pl.ds(s * SLOT_ROWS, SLOT_ROWS)],
                    send_sem=obs_send.at[0],
                    recv_sem=obs_recv.at[s * N_MEM + source],
                    device_id={"mem": source, "col": c},
                    device_id_type=MESH,
                ).wait_recv()

    for copy in loads[LOADS:]:
        copy.wait()
    place = lax.broadcasted_iota(jnp.int32, (1, 2 * SLAB), 1)
    for owner in range(N_MEM):
        for j in range(CD):
            column = sequence[owner * CD + j]
            for layer in range(2):
                r = owner * 2 * CD + layer * CD + j
                pick[r : r + 1, :] = jnp.where(place == column + layer * SLAB, 1.0, 0.0).astype(f32)
    picker = pick[...].astype(bf16)

    @pl.loop(0, LAYERS // 2)
    def _(p):
        pair = prior[pl.ds(p * 2, 2)].reshape(2 * SLAB, LANES)
        chosen = jnp.dot(picker, pair, preferred_element_type=f32).astype(bf16)
        at = pl.ds(pl.multiple_of(p * 2 * CD, 2 * CD), 2 * CD)
        for owner in range(N_MEM):
            states_out[owner, at, :] = chosen[owner * 2 * CD : (owner + 1) * 2 * CD]

    states[m] = states_out[m]

    lane = lax.broadcasted_iota(jnp.int32, (1, BLK), 1)

    def prepare(s):
        for k in range(NPER):
            at = s * SLOT_ROWS + k * BLK
            index = block_index(m, c, s, k)
            region = lax.rem(c + s - 1 + N_COL, N_COL)
            count = counts[region * OBR + index]
            row_w = jnp.where(lane < count, 1.0, 0.0) * lax.rsqrt(variance[s, pl.ds(index, 1), :])
            driven = (departure[s, pl.ds(index, 1), :] * row_w).astype(bf16)
            drive[:, at : at + BLK] = jnp.broadcast_to(driven, (16, BLK))
            column_w = jnp.broadcast_to(row_w, (BLK, BLK)).T
            total = rows[0, at : at + BLK, :].astype(f32)
            for source in range(1, N_MEM):
                total = total + rows[source, at : at + BLK, :].astype(f32)
            mean = jnp.sum(total, axis=1, keepdims=True) * (1.0 / K)
            for source in range(N_MEM):
                tile = ((rows[source, at : at + BLK, :].astype(f32) - mean) * column_w).astype(bf16)
                columns = slice(source * LANES, (source + 1) * LANES)
                scaled[at : at + BLK, columns] = tile
                scaled_t[columns, at : at + BLK] = tile.T

    early, late = slice(0, 2 * SLOT_ROWS), slice(2 * SLOT_ROWS, OBS_ROWS)
    wait_obs(1)
    prepare(1)
    wait_obs(0)
    prepare(0)
    for j in range(NB):
        for i in range(j + 1):
            cross[span(i), span(j)] = jnp.dot(
                scaled_t[span(i), early], scaled[early, span(j)], preferred_element_type=f32
            )
    wait_obs(2)

    state_copies = []
    for q in range(len(STATE_CUTS) - 1):
        low, high = STATE_CUTS[q], STATE_CUTS[q + 1]
        for n, (dz, dk) in enumerate(hops[:-2] + hops[-1:]):
            to_m = member(dz, dk)
            copy = pltpu.make_async_remote_copy(
                src_ref=states_out.at[to_m, pl.ds(low, high - low)],
                dst_ref=states.at[m, pl.ds(low, high - low)],
                send_sem=state_send.at[q * N_MEM + n],
                recv_sem=state_recv.at[q * N_MEM + m],
                device_id={"mem": to_m, "col": c},
                device_id_type=MESH,
            )
            copy.start()
            state_copies.append(copy)

    def wait_states(q):
        low, high = STATE_CUTS[q], STATE_CUTS[q + 1]
        for dz, dk in hops[:-2] + hops[-1:]:
            source = member(dz, dk)
            pltpu.make_async_remote_copy(
                src_ref=states_out.at[source, pl.ds(low, high - low)],
                dst_ref=states.at[source, pl.ds(low, high - low)],
                send_sem=state_send.at[0],
                recv_sem=state_recv.at[q * N_MEM + source],
                device_id={"mem": source, "col": c},
                device_id_type=MESH,
            ).wait_recv()

    prepare(2)
    squares = jnp.zeros((1, B), f32)
    for j in range(NB):
        for i in range(j + 1):
            tile = cross[span(i), span(j)] + jnp.dot(
                scaled_t[span(i), late], scaled[late, span(j)], preferred_element_type=f32
            )
            cross[span(i), span(j)] = tile
            square = jnp.sum(tile * tile, axis=0, keepdims=True)
            squares = squares + (square if i == j else 2.0 * square)
    bound = (K - 1.0) + jnp.sqrt(jnp.sum(squares, axis=1, keepdims=True))
    inverse_bound = 1.0 / bound
    for j in range(NB):
        for i in range(j + 1):
            tile = cross[span(i), span(j)]
            if i == j:
                tile = tile + (K - 1.0) * unit_block()
            tile = (tile * inverse_bound).astype(bf16)
            put_pair(root_a, i, j, tile)
            put_pair(inverse_a, i, j, halved(tile.astype(f32), i == j).astype(bf16))
    projected = jnp.dot(drive[...], scaled[...], preferred_element_type=f32)

    symmetric_dot(root_a, inverse_a, root_b)
    root, spare_root, inverse, spare_inverse = root_b, root_a, inverse_a, inverse_b
    for sweep in range(1, NS_ITERS):
        symmetric_dot(inverse, root, factor, as_factor=True)
        symmetric_dot(factor, inverse, spare_inverse)
        if sweep + 1 < NS_ITERS:
            symmetric_dot(root, factor, spare_root)
        root, spare_root = spare_root, root
        inverse, spare_inverse = spare_inverse, inverse

    half_step = precise_row_times(projected, inverse)
    mean_w = precise_row_times(half_step, inverse) * inverse_bound
    scale = jnp.sqrt((K - 1.0) * inverse_bound)
    weights = factor
    for i in range(N_MEM):
        part = slice(i * LANES, (i + 1) * LANES)
        column = jnp.broadcast_to(mean_w[:1, part], (LANES, LANES)).T
        for j in range(N_MEM):
            other = slice(j * LANES, (j + 1) * LANES)
            weights[part, other] = (scale * inverse[part, other].astype(f32) + column).astype(bf16)

    out_copies = []
    for q in range(len(STATE_CUTS) - 1):
        low, high = STATE_CUTS[q], STATE_CUTS[q + 1]
        wait_states(q)
        total = states[0, low:high, :].astype(f32)
        for source in range(1, N_MEM):
            total = total + states[source, low:high, :].astype(f32)
        mean = jnp.sum(total, axis=1, keepdims=True) * (1.0 / K)
        for source in range(N_MEM):
            columns = slice(source * LANES, (source + 1) * LANES)
            spread[low:high, columns] = (states[source, low:high, :].astype(f32) - mean).astype(bf16)
        for j in range(NB):
            product = jnp.dot(spread[low:high, :], weights[:, span(j)], preferred_element_type=f32)
            result[low:high, span(j)] = (mean + product).astype(bf16)
        cut = pl.ds(low, high - low)
        copy = pltpu.make_async_copy(result.at[cut], out_hbm.at[cut], out_sem.at[q])
        copy.start()
        out_copies.append(copy)
    for copy in out_copies:
        copy.wait()
    for copy in obs_copies + state_copies:
        copy.wait_send()


def body(
    prior_trajectory,
    predicted_measurements,
    departure_vector,
    measurement_error_spread,
    valid_tallies,
    area_point_sequence,
    nearby_batch_map,
):
    anywhere = pl.BlockSpec(memory_space=pl.ANY)
    scalars = pl.BlockSpec(memory_space=pltpu.SMEM)
    matrix = pltpu.VMEM((K, K), bf16)
    partners = 3 * N_MEM - 1
    cuts = len(STATE_CUTS) - 1
    result = pl.pallas_call(
        kernel,
        out_shape=jax.ShapeDtypeStruct((STATE_ROWS, K), bf16),
        in_specs=[anywhere] * 4 + [scalars] * 3,
        out_specs=anywhere,
        scratch_shapes=[
            pltpu.VMEM((LAYERS, SLAB, LANES), bf16),
            pltpu.VMEM((OBR, BLK, LANES), bf16),
            pltpu.VMEM((3, OBR, BLK), f32),
            pltpu.VMEM((3, OBR, BLK), f32),
            pltpu.VMEM((partners, SLOT_ROWS, LANES), bf16),
            pltpu.VMEM((N_MEM, OBS_ROWS, LANES), bf16),
            pltpu.VMEM((N_MEM, STATE_ROWS, LANES), bf16),
            pltpu.VMEM((N_MEM, STATE_ROWS, LANES), bf16),
            pltpu.VMEM((OBS_ROWS, K), bf16),
            pltpu.VMEM((K, OBS_ROWS), bf16),
            pltpu.VMEM((K, K), f32),
            matrix, matrix, matrix, matrix, matrix,
            pltpu.VMEM((STATE_ROWS, K), bf16),
            pltpu.VMEM((STATE_ROWS, K), bf16),
            pltpu.VMEM((2 * SLAB, 2 * SLAB), f32),
            pltpu.VMEM((16, OBS_ROWS), bf16),
            pltpu.SemaphoreType.DMA((LOADS + 7,)),
            pltpu.SemaphoreType.DMA((partners,)),
            pltpu.SemaphoreType.DMA((3 * N_MEM,)),
            pltpu.SemaphoreType.DMA((cuts * N_MEM,)),
            pltpu.SemaphoreType.DMA((cuts * N_MEM,)),
            pltpu.SemaphoreType.DMA((cuts,)),
        ],
        compiler_params=pltpu.CompilerParams(
            collective_id=0, has_side_effects=True, vmem_limit_bytes=56 * 2**20
        ),
        cost_estimate=pl.CostEstimate(flops=32 * 10**9, bytes_accessed=16 * 10**6, transcendentals=0),
    )(
        prior_trajectory,
        predicted_measurements,
        departure_vector,
        measurement_error_spread,
        valid_tallies,
        area_point_sequence,
        jnp.transpose(nearby_batch_map, (1, 2, 0)),
    )
    return result.reshape(LAYERS, CD, K)


def solution(mesh):
    in_specs = (P(None, "col", "mem"), P("col", None, "mem"), P(), P(), P(), P("col"), P())
    out_specs = P(None, ("mem", "col"), None)
    return jax.shard_map(body, mesh=mesh, in_specs=in_specs, out_specs=out_specs, check_vma=False)
```

time: 320 us -> 66.1 us (0.21)
  waiting for transfers between devices: 189 us -> 0 us
  Pallas kernels: 0 us -> 63.2 us
  matrix products: 50 us -> 0 us
  other arithmetic: 35 us -> 0 us
  local copies, waits for them, and re-layouts: 25.1 us -> 2.64 us
  starting transfers between devices: 19.3 us -> 0 us
    ppermute x2 -> x0, waiting for transfers between devices: 165 us -> none  [the longest x1 160 us: extended(): after = lax.ppermute(first, axis, down)]
    pallas_call x0 -> x1, Pallas kernels: none -> 63.2 us  [body(): pl.pallas_call(kernel, out_shape=jax.ShapeDtypeStruct((STATE_ROWS, K), bf...]
    dot_general x16 -> x0, matrix products: 50 us -> none  [the longest x4 15.8 us: analyse(): jnp.dot(factor, inverse, preferred_element_type=jnp.float32)]
    all_to_all x2 -> x0, waiting for transfers between devices: 23.3 us -> none  [the longest x1 23.3 us: body(): lax.all_to_all(chosen, 'mem', split_axis=0, concat_axis=3, tiled=True)]
    gather x5 -> x0, local copies, waits for them, and re-layouts: 21.6 us -> none  [the longest x1 10.7 us: body(): jnp.take(nearby, block_ids, axis=0)]
    concatenate x1 -> x0, other arithmetic: 18.2 us -> none  [extended(): x = jnp.concatenate([before, x, after], axis=dim)]
    all_to_all x2 -> x0, starting transfers between devices: 13.6 us -> none  [the longest x1 7.31 us: body(): lax.all_to_all(chosen, 'mem', split_axis=0, concat_axis=3, tiled=True)]
    select_n x6 -> x0, other arithmetic: 6.96 us -> none  [the longest x2 3.58 us: body(): jnp.take(prior_trajectory, area_point_sequence, axis=1)]
  transfers between devices with their start and end apart: 4 -> 0, of which waited for: 3 -> 0; matrix products, arithmetic and copies ran while one was open for 16% -> 0% of each run, Pallas kernels for 0% -> 0%
where the time goes in v1:
time: 66.1 us; the launch traced here: 65.9 us
  Pallas kernels  63.2 us (96%)
  local copies, waits for them, and re-layouts  2.64 us (4%)
    pallas_call x1, Pallas kernels, body(): pl.pallas_call(kernel, out_shape=jax.ShapeDtypeStruct((STATE_ROWS, K), bf...  63.2 us
    unnamed x1, local copies, waits for them, and re-layouts  2.64 us

profile of v1, /device:TPU:1, one launch (start us, length us, event | category | flops | bytes accessed | tf_op | source)
XLA Modules:
  0.0 65.9 jit_solution(12910889247796879342)
XLA Ops:
  0.0 63.2 %shard_map.73 = bf16[752,1024]{1,0:T(8,128)(2,1)} custom-call(bf16[94,64,128]{2,1,0:T(8,128)(2,1)} %prior_hbm.1, bf16[256,128,128]{2,1,0:T(8,128)(2,1)} %obs_hbm.1, f32[4096,128]{1,0:T(8,128)} %departure_hbm.1, f32[4096,128]{1,0:T(8,128)} %variance_hbm.1, s32[4096]{0:T(1024)} %counts.1, s32[64]{0:T(128)} %sequence.1, s32[3,3,128]{2,1,0:T(4,128)} %bitcast.3), custom_call_target="tpu_custom_call" | custom-call | flops 32000000000 | bytes 16000000 | tf_op jit(solution)/shard_map/pallas_call | solution.py:305
  63.2 2.6 %copy.9 = bf16[94,8,1024]{2,1,0:T(8,128)(2,1)} copy(bf16[94,8,1024]{2,1,0:T(8,128)(2,1)} %bitcast.2) | data formatting | bytes 3080192

commit v2 on v1

--- a/solution.py
+++ b/solution.py
@@ -1,3 +1,5 @@
+import functools
+
 import jax
 import jax.numpy as jnp
 from jax import lax
@@ -42,13 +44,18 @@
     return (3.0 * unit_block() - tile) * 0.5 if diagonal else tile * -0.5
 
 
-def symmetric_dot(a, b, dst, as_factor=False):
+def symmetric_dot(a, b, dst, as_factor=False, beside=()):
+    steps = list(beside)
+    share = -(-len(steps) // (NB * (NB + 1) // 2))
     for j in range(NB):
         for i in range(j + 1):
             tile = jnp.dot(a[span(i), :], b[:, span(j)], preferred_element_type=f32)
             if as_factor:
                 tile = halved(tile, i == j)
             put_pair(dst, i, j, tile.astype(bf16))
+            for step in steps[:share]:
+                step()
+            steps = steps[share:]
 
 
 def precise_row_times(row, matrix):
@@ -64,7 +71,7 @@
 def kernel(
     prior_hbm, obs_hbm, departure_hbm, variance_hbm, counts, sequence, nearby, out_hbm,
     prior, obs, departure, variance, outgoing, rows, states_out, states, scaled, scaled_t,
-    cross, root_a, root_b, inverse_a, inverse_b, factor, spread, result, pick, drive,
+    cross, root_a, root_b, inverse_a, inverse_b, factor, spread, state_mean, result, pick, drive,
     load_sem, obs_send, obs_recv, state_send, state_recv, out_sem,
 ):
     m = lax.axis_index("mem")
@@ -77,13 +84,7 @@
         return lax.rem(m // 2 + dz, 4) * 2 + lax.rem(lax.rem(m, 2) + dk, 2)
 
     hops = [(dz, dk) for dz in (1, 3, 2, 0) for dk in (0, 1)]
-    partners = [(s, dz, dk) for s in (1, 0, 2) for dz, dk in hops if (s, dz, dk) != (1, 0, 0)]
-
-    barrier = pltpu.get_barrier_semaphore()
-    for s, dz, dk in partners:
-        pl.semaphore_signal(
-            barrier, inc=1, device_id={"mem": member(dz, dk), "col": column_of(s)}, device_id_type=MESH
-        )
+    partners = [(s, dz, dk) for dz, dk in hops for s in (1, 0, 2) if (s, dz, dk) != (1, 0, 0)]
 
     loads = []
     part = OBR // LOADS
@@ -96,10 +97,19 @@
         loads.append(pltpu.make_async_copy(departure_hbm.at[cut], departure.at[s], load_sem.at[LOADS + 2 * s]))
         loads.append(pltpu.make_async_copy(variance_hbm.at[cut], variance.at[s], load_sem.at[LOADS + 2 * s + 1]))
     loads.append(pltpu.make_async_copy(prior_hbm, prior, load_sem.at[LOADS + 6]))
-    for copy in loads:
+    for copy in loads[:LOADS]:
         copy.start()
+
+    barrier = pltpu.get_barrier_semaphore()
+    for s, dz, dk in partners:
+        pl.semaphore_signal(
+            barrier, inc=1, device_id={"mem": member(dz, dk), "col": column_of(s)}, device_id_type=MESH
+        )
+
     for copy in loads[:LOADS]:
         copy.wait()
+    for copy in loads[LOADS:]:
+        copy.start()
 
     def block_index(group_m, group_c, s, k):
         return nearby[s, k, group_m * N_COL + group_c]
@@ -182,16 +192,6 @@
 
     early, late = slice(0, 2 * SLOT_ROWS), slice(2 * SLOT_ROWS, OBS_ROWS)
     wait_obs(1)
-    prepare(1)
-    wait_obs(0)
-    prepare(0)
-    for j in range(NB):
-        for i in range(j + 1):
-            cross[span(i), span(j)] = jnp.dot(
-                scaled_t[span(i), early], scaled[early, span(j)], preferred_element_type=f32
-            )
-    wait_obs(2)
-
     state_copies = []
     for q in range(len(STATE_CUTS) - 1):
         low, high = STATE_CUTS[q], STATE_CUTS[q + 1]
@@ -208,6 +208,16 @@
             copy.start()
             state_copies.append(copy)
 
+    prepare(1)
+    wait_obs(0)
+    prepare(0)
+    for j in range(NB):
+        for i in range(j + 1):
+            cross[span(i), span(j)] = jnp.dot(
+                scaled_t[span(i), early], scaled[early, span(j)], preferred_element_type=f32
+            )
+    wait_obs(2)
+
     def wait_states(q):
         low, high = STATE_CUTS[q], STATE_CUTS[q + 1]
         for dz, dk in hops[:-2] + hops[-1:]:
@@ -220,6 +230,21 @@
                 device_id={"mem": source, "col": c},
                 device_id_type=MESH,
             ).wait_recv()
+
+    def centre(low, high):
+        total = states[0, low:high, :].astype(f32)
+        for source in range(1, N_MEM):
+            total = total + states[source, low:high, :].astype(f32)
+        mean = jnp.sum(total, axis=1, keepdims=True) * (1.0 / K)
+        state_mean[low:high, :] = jnp.broadcast_to(mean, (high - low, LANES))
+        for source in range(N_MEM):
+            columns = slice(source * LANES, (source + 1) * LANES)
+            spread[low:high, columns] = (states[source, low:high, :].astype(f32) - mean).astype(bf16)
+
+    def centring(q):
+        wait_states(q)
+        low, high = STATE_CUTS[q], STATE_CUTS[q + 1]
+        return [functools.partial(centre, at, at + 16) for at in range(low, high, 16)]
 
     prepare(2)
     squares = jnp.zeros((1, B), f32)
@@ -246,6 +271,7 @@
     symmetric_dot(root_a, inverse_a, root_b)
     root, spare_root, inverse, spare_inverse = root_b, root_a, inverse_a, inverse_b
     for sweep in range(1, NS_ITERS):
+        last = sweep + 1 == NS_ITERS
         symmetric_dot(inverse, root, factor, as_factor=True)
         symmetric_dot(factor, inverse, spare_inverse)
         if sweep + 1 < NS_ITERS:
@@ -257,26 +283,23 @@
     mean_w = precise_row_times(half_step, inverse) * inverse_bound
     scale = jnp.sqrt((K - 1.0) * inverse_bound)
     weights = factor
+    mean_columns = []
     for i in range(N_MEM):
         part = slice(i * LANES, (i + 1) * LANES)
-        column = jnp.broadcast_to(mean_w[:1, part], (LANES, LANES)).T
-        for j in range(N_MEM):
-            other = slice(j * LANES, (j + 1) * LANES)
-            weights[part, other] = (scale * inverse[part, other].astype(f32) + column).astype(bf16)
-
+        mean_columns.append(jnp.broadcast_to(mean_w[:1, part], (LANES, LANES)).T)
     out_copies = []
     for q in range(len(STATE_CUTS) - 1):
         low, high = STATE_CUTS[q], STATE_CUTS[q + 1]
         wait_states(q)
-        total = states[0, low:high, :].astype(f32)
-        for source in range(1, N_MEM):
-            total = total + states[source, low:high, :].astype(f32)
-        mean = jnp.sum(total, axis=1, keepdims=True) * (1.0 / K)
-        for source in range(N_MEM):
-            columns = slice(source * LANES, (source + 1) * LANES)
-            spread[low:high, columns] = (states[source, low:high, :].astype(f32) - mean).astype(bf16)
+        centre(low, high)
         for j in range(NB):
+            if q == 0:
+                for i in range(N_MEM):
+                    part = slice(i * LANES, (i + 1) * LANES)
+                    column = jnp.concatenate([mean_columns[i]] * (B // LANES), axis=1)
+                    weights[part, span(j)] = (scale * inverse[part, span(j)].astype(f32) + column).astype(bf16)
             product = jnp.dot(spread[low:high, :], weights[:, span(j)], preferred_element_type=f32)
+            mean = jnp.concatenate([state_mean[low:high, :]] * (B // LANES), axis=1)
             result[low:high, span(j)] = (mean + product).astype(bf16)
         cut = pl.ds(low, high - low)
         copy = pltpu.make_async_copy(result.at[cut], out_hbm.at[cut], out_sem.at[q])
@@ -286,6 +309,10 @@
         copy.wait()
     for copy in obs_copies + state_copies:
         copy.wait_send()
+
+
+def pin(x):
+    return pltpu.with_memory_space_constraint(x, pltpu.HBM)
 
 
 def body(
@@ -298,6 +325,7 @@
     nearby_batch_map,
 ):
     anywhere = pl.BlockSpec(memory_space=pl.ANY)
+    in_hbm = pl.BlockSpec(memory_space=pltpu.HBM)
     scalars = pl.BlockSpec(memory_space=pltpu.SMEM)
     matrix = pltpu.VMEM((K, K), bf16)
     partners = 3 * N_MEM - 1
@@ -305,7 +333,7 @@
     result = pl.pallas_call(
         kernel,
         out_shape=jax.ShapeDtypeStruct((STATE_ROWS, K), bf16),
-        in_specs=[anywhere] * 4 + [scalars] * 3,
+        in_specs=[in_hbm] * 4 + [scalars] * 3,
         out_specs=anywhere,
         scratch_shapes=[
             pltpu.VMEM((LAYERS, SLAB, LANES), bf16),
@@ -321,6 +349,7 @@
             pltpu.VMEM((K, K), f32),
             matrix, matrix, matrix, matrix, matrix,
             pltpu.VMEM((STATE_ROWS, K), bf16),
+            pltpu.VMEM((STATE_ROWS, LANES), f32),
             pltpu.VMEM((STATE_ROWS, K), bf16),
             pltpu.VMEM((2 * SLAB, 2 * SLAB), f32),
             pltpu.VMEM((16, OBS_ROWS), bf16),
@@ -332,17 +361,17 @@
             pltpu.SemaphoreType.DMA((cuts,)),
         ],
         compiler_params=pltpu.CompilerParams(
-            collective_id=0, has_side_effects=True, vmem_limit_bytes=56 * 2**20
+            collective_id=0, has_side_effects=True, vmem_limit_bytes=48 * 2**20
         ),
         cost_estimate=pl.CostEstimate(flops=32 * 10**9, bytes_accessed=16 * 10**6, transcendentals=0),
     )(
-        prior_trajectory,
-        predicted_measurements,
-        departure_vector,
-        measurement_error_spread,
-        valid_tallies,
-        area_point_sequence,
-        jnp.transpose(nearby_batch_map, (1, 2, 0)),
+        pin(prior_trajectory),
+        pin(predicted_measurements),
+        pin(departure_vector),
+        pin(measurement_error_spread),
+        pin(valid_tallies),
+        pin(area_point_sequence),
+        pin(jnp.transpose(nearby_batch_map, (1, 2, 0))),
     )
     return result.reshape(LAYERS, CD, K)
 

time: 66.1 us -> 63.4 us (0.959)
  local copies, waits for them, and re-layouts: 2.64 us -> 1.13 us
  Pallas kernels: 63.2 us -> 62.1 us
    unnamed x1, local copies, waits for them, and re-layouts: 2.64 us -> 1.13 us
    pallas_call x1, Pallas kernels: 63.2 us -> 62.1 us  [body(): pl.pallas_call(kernel, out_shape=jax.ShapeDtypeStruct((STATE_ROWS, K), bf...]
where the time goes in v2:
time: 63.4 us; the launch traced here: 63.2 us
  Pallas kernels  62.1 us (98%)
  local copies, waits for them, and re-layouts  1.13 us (2%)
    pallas_call x1, Pallas kernels, body(): pl.pallas_call(kernel, out_shape=jax.ShapeDtypeStruct((STATE_ROWS, K), bf...  62.1 us

profile of v2, /device:TPU:1, one launch (start us, length us, event | category | flops | bytes accessed | tf_op | source)
XLA Modules:
  0.0 63.2 jit_solution(3365718097065795832)
XLA Ops:
  0.0 62.1 %shard_map.73 = bf16[752,1024]{1,0:T(8,128)(2,1)S(1)} custom-call(bf16[94,64,128]{2,1,0:T(8,128)(2,1)} %prior_hbm.1, bf16[256,128,128]{2,1,0:T(8,128)(2,1)} %obs_hbm.1, f32[4096,128]{1,0:T(8,128)} %departure_hbm.1, f32[4096,128]{1,0:T(8,128)} %variance_hbm.1, s32[4096]{0:T(1024)} %counts.1, s32[64]{0:T(128)} %sequence.1, s32[3,3,128]{2,1,0:T(4,128)} %bitcast.3), custom_call_target="tpu_custom_call" | custom-call | flops 32000000000 | bytes 16000000 | tf_op jit(solution)/shard_map/pallas_call | solution.py:333
  62.1 1.1 %copy.9 = bf16[94,8,1024]{2,1,0:T(8,128)(2,1)} copy(bf16[94,8,1024]{2,1,0:T(8,128)(2,1)S(1)} %bitcast.2) | data formatting | bytes 3080192

commit v3 on v2

--- a/solution.py
+++ b/solution.py
@@ -1,5 +1,3 @@
-import functools
-
 import jax
 import jax.numpy as jnp
 from jax import lax
@@ -190,8 +188,8 @@
                 scaled[at : at + BLK, columns] = tile
                 scaled_t[columns, at : at + BLK] = tile.T
 
-    early, late = slice(0, 2 * SLOT_ROWS), slice(2 * SLOT_ROWS, OBS_ROWS)
-    wait_obs(1)
+    for copy in obs_copies[:12]:
+        copy.wait_send()
     state_copies = []
     for q in range(len(STATE_CUTS) - 1):
         low, high = STATE_CUTS[q], STATE_CUTS[q + 1]
@@ -208,14 +206,10 @@
             copy.start()
             state_copies.append(copy)
 
+    wait_obs(1)
     prepare(1)
     wait_obs(0)
     prepare(0)
-    for j in range(NB):
-        for i in range(j + 1):
-            cross[span(i), span(j)] = jnp.dot(
-                scaled_t[span(i), early], scaled[early, span(j)], preferred_element_type=f32
-            )
     wait_obs(2)
 
     def wait_states(q):
@@ -241,18 +235,11 @@
             columns = slice(source * LANES, (source + 1) * LANES)
             spread[low:high, columns] = (states[source, low:high, :].astype(f32) - mean).astype(bf16)
 
-    def centring(q):
-        wait_states(q)
-        low, high = STATE_CUTS[q], STATE_CUTS[q + 1]
-        return [functools.partial(centre, at, at + 16) for at in range(low, high, 16)]
-
     prepare(2)
     squares = jnp.zeros((1, B), f32)
     for j in range(NB):
         for i in range(j + 1):
-            tile = cross[span(i), span(j)] + jnp.dot(
-                scaled_t[span(i), late], scaled[late, span(j)], preferred_element_type=f32
-            )
+            tile = jnp.dot(scaled_t[span(i), :], scaled[:, span(j)], preferred_element_type=f32)
             cross[span(i), span(j)] = tile
             square = jnp.sum(tile * tile, axis=0, keepdims=True)
             squares = squares + (square if i == j else 2.0 * square)
@@ -290,8 +277,14 @@
     out_copies = []
     for q in range(len(STATE_CUTS) - 1):
         low, high = STATE_CUTS[q], STATE_CUTS[q + 1]
-        wait_states(q)
-        centre(low, high)
+        if q == 0:
+            wait_states(0)
+            centre(low, high)
+        following = []
+        if q + 2 < len(STATE_CUTS):
+            wait_states(q + 1)
+            end = STATE_CUTS[q + 2]
+            following = [(at, min(at + 64, end)) for at in range(high, end, 64)]
         for j in range(NB):
             if q == 0:
                 for i in range(N_MEM):
@@ -301,13 +294,15 @@
             product = jnp.dot(spread[low:high, :], weights[:, span(j)], preferred_element_type=f32)
             mean = jnp.concatenate([state_mean[low:high, :]] * (B // LANES), axis=1)
             result[low:high, span(j)] = (mean + product).astype(bf16)
+            if following:
+                centre(*following.pop(0))
         cut = pl.ds(low, high - low)
         copy = pltpu.make_async_copy(result.at[cut], out_hbm.at[cut], out_sem.at[q])
         copy.start()
         out_copies.append(copy)
     for copy in out_copies:
         copy.wait()
-    for copy in obs_copies + state_copies:
+    for copy in obs_copies[12:] + state_copies:
         copy.wait_send()
 
 

time: 63.4 us -> 63.2 us (level)
  no operation moved by 1% of the time
where the time goes in v3:
time: 63.2 us; the launch traced here: 63.1 us
  Pallas kernels  61.9 us (98%)
  local copies, waits for them, and re-layouts  1.13 us (2%)
    pallas_call x1, Pallas kernels, body(): pl.pallas_call(kernel, out_shape=jax.ShapeDtypeStruct((STATE_ROWS, K), bf...  61.9 us

profile of v3, /device:TPU:1, one launch (start us, length us, event | category | flops | bytes accessed | tf_op | source)
XLA Modules:
  0.0 63.1 jit_solution(12729607032991348376)
XLA Ops:
  0.0 61.9 %shard_map.73 = bf16[752,1024]{1,0:T(8,128)(2,1)S(1)} custom-call(bf16[94,64,128]{2,1,0:T(8,128)(2,1)} %prior_hbm.1, bf16[256,128,128]{2,1,0:T(8,128)(2,1)} %obs_hbm.1, f32[4096,128]{1,0:T(8,128)} %departure_hbm.1, f32[4096,128]{1,0:T(8,128)} %variance_hbm.1, s32[4096]{0:T(1024)} %counts.1, s32[64]{0:T(128)} %sequence.1, s32[3,3,128]{2,1,0:T(4,128)} %bitcast.3), custom_call_target="tpu_custom_call" | custom-call | flops 32000000000 | bytes 16000000 | tf_op jit(solution)/shard_map/pallas_call | solution.py:328
  61.9 1.1 %copy.9 = bf16[94,8,1024]{2,1,0:T(8,128)(2,1)} copy(bf16[94,8,1024]{2,1,0:T(8,128)(2,1)S(1)} %bitcast.2) | data formatting | bytes 3080192
